TPU v7x, 32 devices: a whole 2x2x4 slice. The times are simulated.
32 devices in a mesh: col: 4 (over z), leaf: 8 (over y, x, core).
Axes of the slice: x: 2, y: 2, z: 4, core: 2. Of those that a mesh axis runs over, the one named last changes fastest.
Arguments:
- voltage: bfloat16 [128, 32, 4, 1024], P(None, 'leaf', None, 'col'), may hold values from -4 to 4
- source: bfloat16 [128, 32, 4, 1024], P(None, 'leaf', None, 'col'), may hold values from -6 to 6
- conduct: float32 [32, 4, 1024], P('leaf', None, 'col'), may hold values from 0.25 to 2
- leaf_inverse: bfloat16 [32, 4, 1024, 256], P('leaf', None, 'col'), as said below
- update_rows: int32 [4, 32, 4, 2], P('col', 'leaf'), may hold values from 0 to 31, as said below
- update_matrix: bfloat16 [32, 4, 256, 1024], P('leaf', None, None, 'col'), may hold values from -0.1875 to 0.1875
- chain_slot: int32 [16], replicated, may hold values from 0 to 15, as said below
- separator_source: float32 [128, 16, 1024], P(None, 'leaf', 'col'), may hold values from -6 to 6
- separator_inverse: float32 [16, 1024, 256], P('leaf', 'col'), as said below
- separator_coupling: float32 [16, 1024, 256], P('leaf', 'col'), may hold values from -0.3125 to 0.3125
Outputs:
- leaf_result: float32 [128, 32, 4, 1024], P(None, 'leaf', None, 'col')
- separator_result: float32 [128, 16, 1024], P(None, 'leaf', 'col')
Inputs may be any that keep to these rules, and one draw needn't show every extreme that they name: `update_rows`: row [q, x, y] names 2 different update-row blocks of the separator panels at position q; block t holds rows (t % 2) * 128 onward of chain t // 2. Among the 32 entries of the rows [q, x, y] held by one device, at most 4 name blocks whose chains are stored in storage rows i * 2 to (i + 1) * 2 - 1 for one i, and exactly 4 do for some i on every device. A permutation: chain j is stored at row chain_slot[j] of the separator arrays. `leaf_inverse`: each 256 x 256 block is a given inverse of a diagonal block. `separator_inverse`: each 256 x 256 block is a given inverse of a diagonal block.
All inputs are finite; a program needn't handle non-finite values.
Results may differ from a plain program's by a relative error of at most 0.0039.
Values may be sent and summed in bfloat16 or wider, within the bound.
A program may use at most 128 MiB of HBM per device.

v0:
```python
import jax
import jax.numpy as jnp
from jax import lax
from jax.sharding import PartitionSpec as P


def padded_2(shard, sides, width):
    for axis, dim in sides:
        size, length = (lax.axis_size(axis), shard.shape[dim])
        up = [(i, (i + 1) % size) for i in range(size - 1)]
        down = [(j, i) for i, j in up]
        last = lax.slice_in_dim(shard, length - width, length, axis=dim)
        first = lax.slice_in_dim(shard, 0, width, axis=dim)
        before = lax.ppermute(last, axis, up)
        after = lax.ppermute(first, axis, down)
        shard = jnp.concatenate([before, shard, after], axis=dim)
    return shard


def shifted(block, axis, distance):
    devices = range(lax.axis_size(axis))
    route = [(i - distance, i) for i in devices if i - distance in devices]
    return lax.ppermute(block, axis, route)


def body(
    voltage,
    source,
    conduct,
    leaf_inverse,
    update_rows,
    update_matrix,
    chain_slot,
    separator_source,
    separator_inverse,
    separator_coupling,
):
    highest = lax.Precision.HIGHEST
    fields, extent_x, extent_y, panel_width = voltage.shape
    per_leaf = update_rows.shape[3]
    block_rows = update_matrix.shape[2] // per_leaf
    halves = panel_width // block_rows
    panels = extent_x * extent_y
    chains = chain_slot.shape[0]
    sep_rows = separator_source.shape[1]
    padded = padded_2(voltage, (("col", 3), ("leaf", 1)), 1)
    widened = padded.astype(jnp.float32)
    center = widened[:, 1:-1, :, 1:-1]
    beside = widened[:, 2:, :, 1:-1] + widened[:, :-2, :, 1:-1]
    beside = beside + widened[:, 1:-1, :, 2:] + widened[:, 1:-1, :, :-2]
    y_padded = jnp.pad(center, ((0, 0), (0, 0), (1, 1), (0, 0)))
    beside = beside + y_padded[:, :, 2:, :] + y_padded[:, :, :-2, :]
    residual = source.astype(jnp.float32) - ((6.0 + conduct) * center - beside)
    residual_low = residual.astype(jnp.bfloat16).reshape(fields, panels, panel_width)
    inverse = leaf_inverse.reshape(panels, panel_width, panel_width)
    leaf_scaled = jnp.einsum(
        "pab,npb->npa", inverse, residual_low, preferred_element_type=jnp.float32
    )
    blocks = update_matrix.reshape(panels, per_leaf, block_rows, panel_width)
    contrib = jnp.einsum("pkjb,npb->pknj", blocks, residual_low, preferred_element_type=jnp.float32)
    targets = update_rows.reshape(panels, per_leaf)
    chain_hit = (targets // halves)[:, :, None] == jnp.arange(chains, dtype=jnp.int32)
    target_slot = jnp.sum(jnp.where(chain_hit, chain_slot, 0), axis=2)
    target_half = targets % halves
    half_hit = (target_half[:, :, None] == jnp.arange(halves, dtype=jnp.int32)).astype(jnp.float32)
    owners = lax.axis_size("leaf")
    entries = panels * per_leaf
    capacity = max(2, (entries + owners - 1) // owners)
    flat_slot = target_slot.reshape(entries)
    flat_owner = flat_slot // sep_rows
    flat_local = flat_slot % sep_rows * halves + target_half.reshape(entries)
    entry_ids = jnp.arange(entries, dtype=jnp.int32)
    same_owner = flat_owner[:, None] == flat_owner[None, :]
    earlier = entry_ids[None, :] < entry_ids[:, None]
    rank = jnp.sum((same_owner & earlier).astype(jnp.int32), axis=1)
    owner_hit = (flat_owner[None, :] == jnp.arange(owners, dtype=jnp.int32)[:, None]).astype(
        jnp.float32
    )
    rank_hit = (rank[None, :] == jnp.arange(capacity, dtype=jnp.int32)[:, None]).astype(jnp.float32)
    selector = owner_hit[:, None, :] * rank_hit[None, :, :]
    flat_contrib = contrib.reshape(entries, fields, block_rows)
    outgoing = jnp.einsum("dce,enj->dcnj", selector, flat_contrib, precision=highest)
    out_tags = (
        jnp.sum(selector * (flat_local.astype(jnp.float32) + 1.0)[None, None, :], axis=2) - 1.0
    )
    incoming, in_tags = (
        lax.all_to_all(outgoing, "leaf", split_axis=0, concat_axis=0, tiled=True),
        lax.all_to_all(out_tags, "leaf", split_axis=0, concat_axis=0, tiled=True),
    )
    local_hit = (in_tags[:, :, None] == jnp.arange(sep_rows * halves, dtype=jnp.float32)).astype(
        jnp.float32
    )
    gathered = jnp.einsum("scm,scnj->mnj", local_hit, incoming, precision=highest)
    gathered = gathered.reshape(sep_rows, halves, fields, block_rows)
    owned_sums = jnp.transpose(gathered, (0, 2, 1, 3)).reshape(sep_rows, fields, panel_width)
    chain_drive = jnp.transpose(separator_source, (1, 0, 2)) - owned_sums
    column_index = lax.axis_index("col")
    columns = lax.axis_size("col")
    coupling = jnp.where(column_index > 0, separator_coupling, 0.0)

    def push_down(values):
        return jnp.einsum("eab,enb->ena", coupling, values, precision=highest)

    def push_up(values):
        return jnp.einsum("eba,enb->ena", coupling, values, precision=highest)

    def step_down(sweep_turn, values):
        return chain_drive - push_down(shifted(values, "col", 1))

    forward_values = lax.fori_loop(0, columns - 1, step_down, chain_drive)
    chain_scaled = jnp.einsum("eab,enb->ena", separator_inverse, forward_values, precision=highest)

    def step_up(sweep_turn, values):
        return chain_scaled - shifted(push_up(values), "col", -1)

    backward_values = lax.fori_loop(0, columns - 1, step_up, chain_scaled)
    separator_result = jnp.transpose(backward_values, (1, 0, 2))
    separator_low = backward_values.astype(jnp.bfloat16)
    half_low = half_hit.astype(jnp.bfloat16)
    shard_piece = lax.all_gather(separator_low, "leaf", axis=0, tiled=True)
    row_count = shard_piece.shape[0]
    slot_hit = (target_slot[:, :, None] == jnp.arange(row_count, dtype=jnp.int32)).astype(
        jnp.bfloat16
    )
    selector = slot_hit[:, :, :, None] * half_low[:, :, None, :]
    split_rows = shard_piece.reshape(row_count, fields, halves, block_rows)
    picked = jnp.einsum("pksh,snhj->pknj", selector, split_rows, preferred_element_type=jnp.float32)
    correction = jnp.einsum(
        "pkjb,pknj->npb", blocks, picked.astype(jnp.bfloat16), preferred_element_type=jnp.float32
    )
    leaf_result = (leaf_scaled - correction).reshape(fields, extent_x, extent_y, panel_width)
    return (leaf_result, separator_result)


def solution(mesh):
    placed = (
        P(None, "leaf", None, "col"),
        P(None, "leaf", None, "col"),
        P("leaf", None, "col"),
        P("leaf", None, "col", None),
        P("col", "leaf", None, None),
        P("leaf", None, None, "col"),
        P(),
        P(None, "leaf", "col"),
        P("leaf", "col", None),
        P("leaf", "col", None),
    )
    return jax.shard_map(
        body,
        mesh=mesh,
        in_specs=placed,
        out_specs=(P(None, "leaf", None, "col"), P(None, "leaf", "col")),
        check_vma=False,
    )
```

profile of v0, /device:TPU:1, one launch (start us, length us, event | category | flops | bytes accessed | tf_op | source)
XLA Modules:
  0.0 199.6 jit_solution(16748145671829121957)
XLA Ops:
  7.2 2.7 %fusion.33 = (bf16[128,4,4,1]{3,2,1,0:T(4,128)(2,1)}, bf16[128,4,4,1]{3,2,1,0:T(4,128)(2,1)}) fusion(bf16[128,4,4,256]{3,2,1,0:T(4,128)(2,1)} %param.14), kind=kLoop, calls=%fused_computation.76 | loop fusion | bytes 16384 | tf_op jit(solution)/shard_map/slice | solution.py:12
  9.9 4.8 %collective-permute-start.2 = (bf16[128,4,4,1]{3,2,1,0:T(4,128)(2,1)}, bf16[128,4,4,1]{3,2,1,0:T(4,128)(2,1)}, u32[]{:S(2)}, u32[]{:S(2)}) collective-permute-start(bf16[128,4,4,1]{3,2,1,0:T(4,128)(2,1)} %get-tuple-element.76), channel_id=1, source_target_pairs={{0,8},{8,16},{16,24},{1,9},{9,17},{17,25},{2,10},{10,18},{18,26},{... | collective-permute-start | bytes 12296 | tf_op jit(solution)/shard_map/ppermute | solution.py:14
  17.9 6.9 %collective-permute-done.2 = bf16[128,4,4,1]{3,2,1,0:T(4,128)(2,1)} collective-permute-done((bf16[128,4,4,1]{3,2,1,0:T(4,128)(2,1)}, bf16[128,4,4,1]{3,2,1,0:T(4,128)(2,1)}, u32[]{:S(2)}, u32[]{:S(2)}) %collective-permute-start.2) | collective-permute-done | bytes 4128 | tf_op jit(solution)/shard_map/ppermute | solution.py:14
  24.8 4.6 %collective-permute-done.3 = bf16[128,4,4,1]{3,2,1,0:T(4,128)(2,1)} collective-permute-done((bf16[128,4,4,1]{3,2,1,0:T(4,128)(2,1)}, bf16[128,4,4,1]{3,2,1,0:T(4,128)(2,1)}, u32[]{:S(2)}, u32[]{:S(2)}) %collective-permute-start.3) | collective-permute-done | bytes 4128 | tf_op jit(solution)/shard_map/ppermute | solution.py:15
  29.4 2.7 %pad_maximum_fusion.2 = (bf16[128,1,4,258]{3,2,1,0:T(4,128)(2,1)}, bf16[128,1,4,258]{3,2,1,0:T(4,128)(2,1)S(1)}) fusion(bf16[128,4,4,1]{3,2,1,0:T(4,128)(2,1)} %collective-permute-done.3, bf16[128,4,4,256]{3,2,1,0:T(4,128)(2,1)S(1)} %copy-done.3, bf16[128,4,4,1]{3,2,1,0:T(4,128)(2,1)} %collective-permute-done.2), kind=kLoop, calls=%fused_computation.27 | loop fusion | flops 1585152 | bytes 1585152 | tf_op jit(solution)/shard_map/slice | solution.py:12
  32.1 4.9 %collective-permute-start.4 = (bf16[128,1,4,258]{3,2,1,0:T(4,128)(2,1)}, bf16[128,1,4,258]{3,2,1,0:T(4,128)(2,1)}, u32[]{:S(2)}, u32[]{:S(2)}) collective-permute-start(bf16[128,1,4,258]{3,2,1,0:T(4,128)(2,1)} %get-tuple-element.74), channel_id=1, source_target_pairs={{0,1},{1,2},{2,3},{3,4},{4,5},{5,6},{6,7},{8,9},{9,10},{10,11},{11... | collective-permute-start | bytes 792584 | tf_op jit(solution)/shard_map/ppermute | solution.py:14
  40.9 4.4 %all-to-all-start = ((f32[8,1,4]{2,1,0:T(1,128)}), f32[8,1,4]{2,1,0:T(1,128)}, u32[]{:S(2)}, u32[]{:S(2)}) async-start(f32[8,1,4]{2,1,0:T(1,128)} %copy.71), calls=%async_computation | async-start | bytes 8192 | tf_op jit(solution)/shard_map/all_to_all | solution.py:88
  48.2 3.7 %maximum_convert_fusion = f32[128,6,4,258]{3,2,1,0:T(4,128)S(1)} fusion(bf16[128,1,4,258]{3,2,1,0:T(4,128)(2,1)} %collective-permute-done.5, bf16[128,4,4,1]{3,2,1,0:T(4,128)(2,1)} %collective-permute-done.3, bf16[128,4,4,256]{3,2,1,0:T(4,128)(2,1)S(1)} %copy-done.3, bf16[128,4,4,1]{3,2,1,0:T(4,128)(2,1)} %collective-permute-done.2, ...), kind=kLoop, calls=%fused_computation.3 | loop fusion | flops 7925760 | bytes 4755456 | tf_op jit(solution)/shard_map/convert_element_type | solution.py:47
  53.1 4.3 %fusion.4 = bf16[128,4,4,256]{3,2,1,0:T(4,128)(2,1)} fusion(f32[128,4,4,256]{3,2,1,0:T(4,128)S(1)} %slice.44, f32[128,6,4,258]{3,2,1,0:T(4,128)S(1)} %maximum_convert_fusion, bf16[128,4,4,256]{3,2,1,0:T(4,128)(2,1)S(1)} %copy-done.5, f32[4,4,256]{2,1,0:T(4,128)S(1)} %broadcast_add_fusion), kind=kLoop, calls=%fused_computation.8 | loop fusion | flops 5242880 | bytes 12599296 | tf_op jit(solution)/shard_map/convert_element_type | solution.py:54
  59.7 5.1 %fusion.5 = f32[8,4,128,128]{3,1,2,0:T(4,128)} fusion(f32[32,128,128]{2,1,0:T(8,128)S(1)} %bitcast.71, f32[8,4,32,1]{2,0,1,3:T(8,128)S(1)} %get-tuple-element.79), kind=kOutput, calls=%fused_computation.14 | convolution fusion | flops 201326592 | bytes 4198400 | tf_op jit(solution)/shard_map/dce,enj->dcnj/dot_general | solution.py:82
  64.8 4.4 %all-to-all-start.1 = ((f32[8,4,128,128]{3,1,2,0:T(4,128)}), f32[8,4,128,128]{3,1,2,0:T(4,128)}, u32[]{:S(2)}, u32[]{:S(2)}) async-start(f32[8,4,128,128]{3,1,2,0:T(4,128)} %fusion.5), calls=%async_computation.1 | async-start | bytes 4194304 | tf_op jit(solution)/shard_map/all_to_all | solution.py:87
  70.3 21.0 %all-to-all-done.1 = f32[8,4,128,128]{3,1,2,0:T(4,128)} async-done(((f32[8,4,128,128]{3,1,2,0:T(4,128)}), f32[8,4,128,128]{3,1,2,0:T(4,128)}, u32[]{:S(2)}, u32[]{:S(2)}) %all-to-all-start.1) | async-done | bytes 2097184 | tf_op jit(solution)/shard_map/all_to_all | solution.py:87
  91.4 3.6 %fusion.7 = f32[4,128,128,1]{2,0,3,1:T(4,128)S(1)} fusion(f32[8,4,128,128]{3,1,2,0:T(4,128)} %all-to-all-done.1, f32[8,4]{0,1:T(4,128)S(1)} %bitcast.76), kind=kOutput, calls=%fused_computation.16 | convolution fusion | flops 25165952 | bytes 2359424 | tf_op jit(solution)/shard_map/scm,scnj->mnj/dot_general | solution.py:93
  95.3 21.9 %while.20 = (s32[]{:T(128)}, f32[2,128,256]{2,1,0:T(8,128)S(1)}, f32[2,256,256]{2,1,0:T(8,128)S(1)}, f32[2,128,256]{2,1,0:T(8,128)S(1)}, s32[]{:T(128)}) while((s32[]{:T(128)}, f32[2,128,256]{2,1,0:T(8,128)S(1)}, f32[2,256,256]{2,1,0:T(8,128)S(1)}, f32[2,128,256]{2,1,0:T(8,128)S(1)}, s32[]{:T(128)}) %tuple.44), condition=%wide.region_4.5_spmd, body=%wide.region_3.4_spmd.sunk | while | flops 201392128 | bytes 2359397 | solution.py:110
  97.8 3.3 %collective-permute-done = f32[2,128,256]{2,1,0:T(8,128)S(1)} collective-permute-done((f32[2,128,256]{2,1,0:T(8,128)S(1)}, f32[2,128,256]{2,1,0:T(8,128)S(1)}, u32[]{:S(2)}, u32[]{:S(2)}) %collective-permute-start) | collective-permute-done | bytes 262176 | tf_op jit(solution)/shard_map/while/body/eval_jaxpr/ppermute | solution.py:23
  101.7 3.8 %collective-permute-start = (f32[2,128,256]{2,1,0:T(8,128)S(1)}, f32[2,128,256]{2,1,0:T(8,128)S(1)}, u32[]{:S(2)}, u32[]{:S(2)}) collective-permute-start(f32[2,128,256]{2,1,0:T(8,128)S(1)} %get-tuple-element.138), channel_id=1, source_target_pairs={{0,8},{8,16},{16,24},{1,9},{9,17},{17,25},{2,10},{10,18},{18,26},{... | collective-permute-start | bytes 786440 | tf_op jit(solution)/shard_map/while/body/eval_jaxpr/ppermute | solution.py:23
  105.6 3.3 %collective-permute-done = f32[2,128,256]{2,1,0:T(8,128)S(1)} collective-permute-done((f32[2,128,256]{2,1,0:T(8,128)S(1)}, f32[2,128,256]{2,1,0:T(8,128)S(1)}, u32[]{:S(2)}, u32[]{:S(2)}) %collective-permute-start) | collective-permute-done | bytes 262176 | tf_op jit(solution)/shard_map/while/body/eval_jaxpr/ppermute | solution.py:23
  109.5 3.8 %collective-permute-start = (f32[2,128,256]{2,1,0:T(8,128)S(1)}, f32[2,128,256]{2,1,0:T(8,128)S(1)}, u32[]{:S(2)}, u32[]{:S(2)}) collective-permute-start(f32[2,128,256]{2,1,0:T(8,128)S(1)} %get-tuple-element.138), channel_id=1, source_target_pairs={{0,8},{8,16},{16,24},{1,9},{9,17},{17,25},{2,10},{10,18},{18,26},{... | collective-permute-start | bytes 786440 | tf_op jit(solution)/shard_map/while/body/eval_jaxpr/ppermute | solution.py:23
  113.4 3.3 %collective-permute-done = f32[2,128,256]{2,1,0:T(8,128)S(1)} collective-permute-done((f32[2,128,256]{2,1,0:T(8,128)S(1)}, f32[2,128,256]{2,1,0:T(8,128)S(1)}, u32[]{:S(2)}, u32[]{:S(2)}) %collective-permute-start) | collective-permute-done | bytes 262176 | tf_op jit(solution)/shard_map/while/body/eval_jaxpr/ppermute | solution.py:23
  119.0 29.6 %while.21 = (s32[]{:T(128)}, f32[2,128,256]{2,1,0:T(8,128)S(1)}, f32[2,256,256]{2,1,0:T(8,128)S(1)}, f32[2,128,256]{2,1,0:T(8,128)S(1)}, s32[]{:T(128)}) while((s32[]{:T(128)}, f32[2,128,256]{2,1,0:T(8,128)S(1)}, f32[2,256,256]{2,1,0:T(8,128)S(1)}, f32[2,128,256]{2,1,0:T(8,128)S(1)}, s32[]{:T(128)}) %tuple.52), condition=%wide.region_6.7_spmd, body=%wide.region_5.6_spmd.sunk | while | flops 201392128 | bytes 2883685 | solution.py:116
  121.5 6.5 %collective-permute-done.1 = f32[2,128,256]{2,1,0:T(8,128)S(1)} collective-permute-done((f32[2,128,256]{2,1,0:T(8,128)}, f32[2,128,256]{2,1,0:T(8,128)S(1)}, u32[]{:S(2)}, u32[]{:S(2)}) %collective-permute-start.1) | collective-permute-done | bytes 262176 | tf_op jit(solution)/shard_map/while/body/eval_jaxpr/ppermute | solution.py:23
  130.4 7.1 %collective-permute-done.1 = f32[2,128,256]{2,1,0:T(8,128)S(1)} collective-permute-done((f32[2,128,256]{2,1,0:T(8,128)}, f32[2,128,256]{2,1,0:T(8,128)S(1)}, u32[]{:S(2)}, u32[]{:S(2)}) %collective-permute-start.1) | collective-permute-done | bytes 262176 | tf_op jit(solution)/shard_map/while/body/eval_jaxpr/ppermute | solution.py:23
  140.1 8.5 %collective-permute-done.1 = f32[2,128,256]{2,1,0:T(8,128)S(1)} collective-permute-done((f32[2,128,256]{2,1,0:T(8,128)}, f32[2,128,256]{2,1,0:T(8,128)S(1)}, u32[]{:S(2)}, u32[]{:S(2)}) %collective-permute-start.1) | collective-permute-done | bytes 262176 | tf_op jit(solution)/shard_map/while/body/eval_jaxpr/ppermute | solution.py:23
  150.3 32.0 %all-gather.2.cloned.1.call-done = bf16[16,128,256]{2,1,0:T(8,128)(2,1)} async-done(((bf16[2,128,256]{2,1,0:T(8,128)(2,1)}), bf16[16,128,256]{2,1,0:T(8,128)(2,1)}) %all-gather.2.cloned.1.call-update) | async-done | bytes 1048592 | tf_op jit(solution)/shard_map/all_gather | solution.py:120
  (83 shorter events, 40.4 us)
Async XLA Ops:
  7.2 51.6 %copy-start = (bf16[4,4,256,256]{3,2,1,0:T(8,128)(2,1)S(1)}, bf16[4,4,256,256]{3,2,1,0:T(8,128)(2,1)}, u32[]{:S(2)}) copy-start(bf16[4,4,256,256]{3,2,1,0:T(8,128)(2,1)} %param.19) | copy-start | bytes 6291460
  7.2 22.2 %copy-start.3 = (bf16[128,4,4,256]{3,2,1,0:T(4,128)(2,1)S(1)}, bf16[128,4,4,256]{3,2,1,0:T(4,128)(2,1)}, u32[]{:S(2)}) copy-start(bf16[128,4,4,256]{3,2,1,0:T(4,128)(2,1)} %param.14) | copy-start | bytes 3145732
  7.2 8.8 %copy-start.8 = (s32[1,4,4,2]{2,3,1,0:T(2,128)S(1)}, s32[1,4,4,2]{2,3,1,0:T(2,128)}, u32[]{:S(2)}) copy-start(s32[1,4,4,2]{2,3,1,0:T(2,128)} %param.18) | copy-start | bytes 388
  7.2 9.5 %copy-start.12 = (s32[16]{0:T(128)S(1)}, s32[16]{0:T(128)}, u32[]{:S(2)}) copy-start(s32[16]{0:T(128)} %param.20) | copy-start | bytes 196
  9.9 14.9 %collective-permute-start.2 = (bf16[128,4,4,1]{3,2,1,0:T(4,128)(2,1)}, bf16[128,4,4,1]{3,2,1,0:T(4,128)(2,1)}, u32[]{:S(2)}, u32[]{:S(2)}) collective-permute-start(bf16[128,4,4,1]{3,2,1,0:T(4,128)(2,1)} %get-tuple-element.76), channel_id=1, source_target_pairs={{0,8},{8,16},{16,24},{1,9},{9,17},{17,25},{2,10},{10,18},{18,26},{... | collective-permute-start | bytes 12296 | tf_op jit(solution)/shard_map/ppermute | solution.py:14
  14.7 14.7 %collective-permute-start.3 = (bf16[128,4,4,1]{3,2,1,0:T(4,128)(2,1)}, bf16[128,4,4,1]{3,2,1,0:T(4,128)(2,1)}, u32[]{:S(2)}, u32[]{:S(2)}) collective-permute-start(bf16[128,4,4,1]{3,2,1,0:T(4,128)(2,1)} %get-tuple-element.77), channel_id=1, source_target_pairs={{8,0},{16,8},{24,16},{9,1},{17,9},{25,17},{10,2},{18,10},{26,18},{... | collective-permute-start | bytes 12296 | tf_op jit(solution)/shard_map/ppermute | solution.py:15
  32.1 13.8 %collective-permute-start.4 = (bf16[128,1,4,258]{3,2,1,0:T(4,128)(2,1)}, bf16[128,1,4,258]{3,2,1,0:T(4,128)(2,1)}, u32[]{:S(2)}, u32[]{:S(2)}) collective-permute-start(bf16[128,1,4,258]{3,2,1,0:T(4,128)(2,1)} %get-tuple-element.74), channel_id=1, source_target_pairs={{0,1},{1,2},{2,3},{3,4},{4,5},{5,6},{6,7},{8,9},{9,10},{10,11},{11... | collective-permute-start | bytes 792584 | tf_op jit(solution)/shard_map/ppermute | solution.py:14
  37.0 11.2 %collective-permute-start.5 = (bf16[128,1,4,258]{3,2,1,0:T(4,128)(2,1)S(1)}, bf16[128,1,4,258]{3,2,1,0:T(4,128)(2,1)}, u32[]{:S(2)}, u32[]{:S(2)}) collective-permute-start(bf16[128,1,4,258]{3,2,1,0:T(4,128)(2,1)S(1)} %get-tuple-element.75), channel_id=1, source_target_pairs={{1,0},{2,1},{3,2},{4,3},{5,4},{6,5},{7,6},{9,8},{10,9},{11,10},{12... | collective-permute-start | bytes 792584 | tf_op jit(solution)/shard_map/ppermute | solution.py:15
  40.9 24.0 %all-to-all-start = ((f32[8,1,4]{2,1,0:T(1,128)}), f32[8,1,4]{2,1,0:T(1,128)}, u32[]{:S(2)}, u32[]{:S(2)}) async-start(f32[8,1,4]{2,1,0:T(1,128)} %copy.71), calls=%async_computation | async-start | bytes 8192 | tf_op jit(solution)/shard_map/all_to_all | solution.py:88
  51.9 1.2 copy-start.5
  64.8 4.7 %copy-start.6 = (f32[2,256,256]{2,1,0:T(8,128)S(1)}, f32[2,256,256]{2,1,0:T(8,128)}, u32[]{:S(2)}) copy-start(f32[2,256,256]{2,1,0:T(8,128)} %param.23) | copy-start | bytes 1572868
  64.8 26.5 %all-to-all-start.1 = ((f32[8,4,128,128]{3,1,2,0:T(4,128)}), f32[8,4,128,128]{3,1,2,0:T(4,128)}, u32[]{:S(2)}, u32[]{:S(2)}) async-start(f32[8,4,128,128]{3,1,2,0:T(4,128)} %fusion.5), calls=%async_computation.1 | async-start | bytes 4194304 | tf_op jit(solution)/shard_map/all_to_all | solution.py:87
  69.3 26.0 %copy-start.7 = (f32[128,2,256]{2,1,0:T(2,128)S(1)}, f32[128,2,256]{2,1,0:T(2,128)}, u32[]{:S(2)}) copy-start(f32[128,2,256]{2,1,0:T(2,128)} %param.21) | copy-start | bytes 786436
  69.3 113.0 %all-gather.2.cloned.1.call-start = ((), (), s32[]{:S(2)}) async-start(), calls=%async_computation.2 | async-start | bytes 1179648 | tf_op jit(solution)/shard_map/all_gather | solution.py:120
  95.4 5.7 %collective-permute-start = (f32[2,128,256]{2,1,0:T(8,128)S(1)}, f32[2,128,256]{2,1,0:T(8,128)S(1)}, u32[]{:S(2)}, u32[]{:S(2)}) collective-permute-start(f32[2,128,256]{2,1,0:T(8,128)S(1)} %get-tuple-element.138), channel_id=1, source_target_pairs={{0,8},{8,16},{16,24},{1,9},{9,17},{17,25},{2,10},{10,18},{18,26},{... | collective-permute-start | bytes 786440 | tf_op jit(solution)/shard_map/while/body/eval_jaxpr/ppermute | solution.py:23
  101.7 7.1 %collective-permute-start = (f32[2,128,256]{2,1,0:T(8,128)S(1)}, f32[2,128,256]{2,1,0:T(8,128)S(1)}, u32[]{:S(2)}, u32[]{:S(2)}) collective-permute-start(f32[2,128,256]{2,1,0:T(8,128)S(1)} %get-tuple-element.138), channel_id=1, source_target_pairs={{0,8},{8,16},{16,24},{1,9},{9,17},{17,25},{2,10},{10,18},{18,26},{... | collective-permute-start | bytes 786440 | tf_op jit(solution)/shard_map/while/body/eval_jaxpr/ppermute | solution.py:23
  109.5 7.1 %collective-permute-start = (f32[2,128,256]{2,1,0:T(8,128)S(1)}, f32[2,128,256]{2,1,0:T(8,128)S(1)}, u32[]{:S(2)}, u32[]{:S(2)}) collective-permute-start(f32[2,128,256]{2,1,0:T(8,128)S(1)} %get-tuple-element.138), channel_id=1, source_target_pairs={{0,8},{8,16},{16,24},{1,9},{9,17},{17,25},{2,10},{10,18},{18,26},{... | collective-permute-start | bytes 786440 | tf_op jit(solution)/shard_map/while/body/eval_jaxpr/ppermute | solution.py:23
  119.0 30.3 %copy-start.11 = (s32[16,2]{0,1:T(2,128)S(1)}, s32[16,2]{0,1:T(2,128)}, u32[]{:S(2)}) copy-start(s32[16,2]{0,1:T(2,128)} %get-tuple-element.80) | copy-start | bytes 388
  119.0 30.3 %copy-start.10 = (s32[16,2]{0,1:T(2,128)S(1)}, s32[16,2]{0,1:T(2,128)}, u32[]{:S(2)}) copy-start(s32[16,2]{0,1:T(2,128)} %copy-done.9) | copy-start | bytes 388
  120.2 7.8 %collective-permute-start.1 = (f32[2,128,256]{2,1,0:T(8,128)}, f32[2,128,256]{2,1,0:T(8,128)S(1)}, u32[]{:S(2)}, u32[]{:S(2)}) collective-permute-start(f32[2,128,256]{2,1,0:T(8,128)} %fusion.54), channel_id=1, source_target_pairs={{8,0},{16,8},{24,16},{9,1},{17,9},{25,17},{10,2},{18,10},{26,18},{... | collective-permute-start | bytes 786440 | tf_op jit(solution)/shard_map/while/body/eval_jaxpr/ppermute | solution.py:23
  129.2 8.4 %collective-permute-start.1 = (f32[2,128,256]{2,1,0:T(8,128)}, f32[2,128,256]{2,1,0:T(8,128)S(1)}, u32[]{:S(2)}, u32[]{:S(2)}) collective-permute-start(f32[2,128,256]{2,1,0:T(8,128)} %fusion.54), channel_id=1, source_target_pairs={{8,0},{16,8},{24,16},{9,1},{17,9},{25,17},{10,2},{18,10},{26,18},{... | collective-permute-start | bytes 786440 | tf_op jit(solution)/shard_map/while/body/eval_jaxpr/ppermute | solution.py:23
  138.8 9.8 %collective-permute-start.1 = (f32[2,128,256]{2,1,0:T(8,128)}, f32[2,128,256]{2,1,0:T(8,128)S(1)}, u32[]{:S(2)}, u32[]{:S(2)}) collective-permute-start(f32[2,128,256]{2,1,0:T(8,128)} %fusion.54), channel_id=1, source_target_pairs={{8,0},{16,8},{24,16},{9,1},{17,9},{25,17},{10,2},{18,10},{26,18},{... | collective-permute-start | bytes 786440 | tf_op jit(solution)/shard_map/while/body/eval_jaxpr/ppermute | solution.py:23
  187.4 1.2 copy-start.2
  187.4 1.9 copy-start.4
  (2 other events, 1.5 us)
Sparse Core Ops, SparseCore 0:
  149.4 32.8 all-gather.1
where the time goes:
time: 201 us; the launch traced here: 200 us
  waiting for transfers between devices  98.7 us (49%)
  starting transfers between devices  35.8 us (18%)
  matrix products  19.6 us (10%)
  local copies, waits for them, and re-layouts  17 us (8%)
  between operations  14.3 us (7%)
  other arithmetic  14 us (7%)
    ppermute x6, waiting for transfers between devices, shifted(): return lax.ppermute(block, axis, route)  32 us
    all_gather x1, waiting for transfers between devices, body(): shard_piece = lax.all_gather(separator_low, 'leaf', axis=0, tiled=True)  32 us
    all_to_all x1, waiting for transfers between devices, body(): lax.all_to_all(outgoing, 'leaf', split_axis=0, concat_axis=0, tiled=True)  21 us
    ppermute x6, starting transfers between devices, shifted(): return lax.ppermute(block, axis, route)  13.9 us
    ppermute x2, starting transfers between devices, padded_2(): before = lax.ppermute(last, axis, up)  9.68 us
    ppermute x2, waiting for transfers between devices, padded_2(): before = lax.ppermute(last, axis, up)  6.94 us
    ppermute x2, waiting for transfers between devices, padded_2(): after = lax.ppermute(first, axis, down)  6.78 us
    dot_general x1, matrix products, body(): jnp.einsum('dce,enj->dcnj', selector, flat_contrib, precision=highest)  5.1 us
  transfers between devices with their start and end apart: 13, of which 11 were waited for; matrix products, arithmetic and copies ran while one was open for 11% of the time, Pallas kernels for 0%

commit v1 on v0

v1 whole, which is shorter than its diff:
```python
import functools
import jax
import jax.numpy as jnp
from jax import lax
from jax.experimental import pallas as pl
from jax.experimental.pallas import tpu as pltpu
from jax.sharding import PartitionSpec as P

F32 = jnp.float32
BF16 = jnp.bfloat16
SPLIT = 2
PAIR = F32
HOP = BF16
NT = (((1,), (1,)), ((), ()))
NN = (((1,), (0,)), ((), ()))


def flipped(value, bits, count):
    total = 0
    weight = 1
    while weight < count:
        digit = (value // weight) % 2
        total = total + weight * (1 - digit if (bits // weight) % 2 else digit)
        weight *= 2
    return total


def dot(left, right, dims):
    return lax.dot_general(left, right, dims, preferred_element_type=F32)


def halved(value):
    high = value.astype(BF16)
    return high, (value - high.astype(F32)).astype(BF16)


def kernel(
    n_leaf, n_col, cap, extent_x, extent_y, sep_rows, halves,
    tab, v, s, cond, sep, inv_hbm, upd_hbm, sinv_hbm, coup_hbm,
    out, res,
    inv, upd, sinv, coup, c_hi, c_lo, d_hi, d_lo,
    resid, contrib, z_send, z_recv, x_recv,
    pair_send, pair_recv, keep, chip_send, chip_recv,
    drive, f_send, f_recv, scaled, b_send, b_recv, gath,
    load_sem, zs_sem, zr_sem, xs_sem, xr_sem, ps_sem, pr_sem, cs_sem, cr_sem,
    fs_sem, fr_sem, bs_sem, br_sem, gs_sem, gr_sem, hs_sem, hr_sem,
):
    panels, fields, width = v.shape
    block = width // halves
    local = sep_rows * halves
    chips = n_leaf // 2
    leaf = lax.axis_index("leaf")
    col = lax.axis_index("col")
    core = leaf % 2
    chip = leaf // 2
    sibling = chip * 2 + (1 - core)
    entries = 2 * panels
    owners_cap = n_leaf * cap
    MESH = pl.DeviceIdType.MESH

    def remote(src, dst, send, recv, target):
        return pltpu.make_async_remote_copy(
            src_ref=src, dst_ref=dst, send_sem=send, recv_sem=recv,
            device_id=target, device_id_type=MESH,
        )

    loads = [
        pltpu.make_async_copy(src, dst, load_sem.at[i])
        for i, (src, dst) in enumerate(
            ((upd_hbm, upd), (inv_hbm, inv), (coup_hbm, coup), (sinv_hbm, sinv))
        )
    ]
    for load in loads:
        load.start()

    barrier = pltpu.get_barrier_semaphore()
    for step in range(1, n_leaf):
        pl.semaphore_signal(
            barrier, inc=1, device_id={"leaf": (leaf + step) % n_leaf}, device_id_type=MESH
        )
    has_below, has_above = col > 0, col < n_col - 1
    leaf_below, leaf_above = leaf > 0, leaf < n_leaf - 1

    @pl.when(has_below)
    def _():
        pl.semaphore_signal(barrier, inc=1, device_id={"col": col - 1}, device_id_type=MESH)

    @pl.when(has_above)
    def _():
        pl.semaphore_signal(barrier, inc=1, device_id={"col": col + 1}, device_id_type=MESH)

    lane = lax.broadcasted_iota(jnp.int32, (fields, 128), 1)
    first = jnp.zeros((fields, 128), F32)
    last = jnp.zeros((fields, 128), F32)
    for p in range(panels):
        first = jnp.where(lane == p, v[p, :, 0:128].astype(F32)[:, 0:1], first)
        last = jnp.where(lane == p, v[p, :, width - 128:].astype(F32)[:, 127:128], last)
    z_send[0] = first.astype(BF16)
    z_send[1] = last.astype(BF16)

    beside_col = (col + n_col - 1) // n_col + (2 * n_col - 2 - col) // n_col
    pl.semaphore_wait(barrier, n_leaf - 1 + beside_col)

    z_down = lambda: remote(z_send.at[0], z_recv.at[1], zs_sem.at[0], zr_sem.at[1], {"col": col - 1})
    z_up = lambda: remote(z_send.at[1], z_recv.at[0], zs_sem.at[1], zr_sem.at[0], {"col": col + 1})
    x_down = lambda: remote(
        v.at[pl.ds(0, extent_y)], x_recv.at[1], xs_sem.at[0], xr_sem.at[1], {"leaf": leaf - 1}
    )
    x_up = lambda: remote(
        v.at[pl.ds(panels - extent_y, extent_y)], x_recv.at[0], xs_sem.at[1], xr_sem.at[0],
        {"leaf": leaf + 1},
    )

    for has, copy in ((has_below, z_down), (has_above, z_up), (leaf_below, x_down), (leaf_above, x_up)):
        @pl.when(has)
        def _(copy=copy):
            copy().start()

    for has, ref, slot in (
        (has_below, z_recv, 0), (has_above, z_recv, 1), (leaf_below, x_recv, 0), (leaf_above, x_recv, 1),
    ):
        @pl.when(jnp.logical_not(has))
        def _(ref=ref, slot=slot):
            ref[slot] = jnp.zeros(ref.shape[1:], ref.dtype)

    @pl.when(has_below)
    def _():
        z_up().wait_recv()

    @pl.when(has_above)
    def _():
        z_down().wait_recv()

    loads[0].wait()
    wide_lane = lax.broadcasted_iota(jnp.int32, (fields, width), 1)

    def residual_panel(x, y):
        p = x * extent_y + y
        center = v[p].astype(F32)
        before = z_recv[0].astype(F32)[:, p:p + 1]
        after = z_recv[1].astype(F32)[:, p:p + 1]
        beside = jnp.where(wide_lane == 0, before, pltpu.roll(center, 1, 1))
        beside = beside + jnp.where(wide_lane == width - 1, after, pltpu.roll(center, width - 1, 1))
        beside = beside + (v[p - extent_y] if x > 0 else x_recv[0, y]).astype(F32)
        beside = beside + (v[p + extent_y] if x < extent_x - 1 else x_recv[1, y]).astype(F32)
        if y > 0:
            beside = beside + v[p - 1].astype(F32)
        if y < extent_y - 1:
            beside = beside + v[p + 1].astype(F32)
        low = (s[p].astype(F32) - ((6.0 + cond[p:p + 1, :]) * center - beside)).astype(BF16)
        resid[p] = low
        product = dot(low, upd[p], NT)
        contrib[2 * p] = product[:, :block]
        contrib[2 * p + 1] = product[:, block:]

    for x in range(1, extent_x - 1):
        for y in range(extent_y):
            residual_panel(x, y)

    @pl.when(leaf_below)
    def _():
        x_up().wait_recv()

    @pl.when(leaf_above)
    def _():
        x_down().wait_recv()

    for x in (0, extent_x - 1):
        for y in range(extent_y):
            residual_panel(x, y)

    def dense(owner, m):
        total = jnp.zeros((fields, block), F32)
        for r in range(cap):
            at = owner * cap + r
            weight = jnp.where(tab[owners_cap + at] == m, 1.0, 0.0).astype(F32)
            total = total + weight * contrib[tab[at]]
        return total

    order = list(range(chips - 1, -1, -1))
    peer_chip = [flipped(chip, d, chips) for d in range(chips)]

    def pair_copy(d):
        return remote(pair_send.at[d], pair_recv.at[d], ps_sem.at[d], pr_sem.at[d], {"leaf": sibling})

    def chip_copy(d):
        return remote(
            chip_send.at[d], chip_recv.at[d], cs_sem.at[d], cr_sem.at[d],
            {"leaf": peer_chip[d] * 2 + core},
        )

    for d in order:
        def fill(m, carry, d=d):
            pair_send[d, m] = dense(peer_chip[d] * 2 + (1 - core), m).astype(pair_send.dtype)
            return carry
        lax.fori_loop(0, local, fill, 0)
        pair_copy(d).start()
    for d in order:
        def fill_own(m, carry, d=d):
            keep[d, m] = dense(peer_chip[d] * 2 + core, m)
            return carry
        lax.fori_loop(0, local, fill_own, 0)
        pair_copy(d).wait_recv()
        if d > 0:
            chip_send[d] = (keep[d] + pair_recv[d].astype(F32)).astype(BF16)
            chip_copy(d).start()

    for load in loads[1:]:
        load.wait()

    def leaf_scale(p, carry):
        out[p] = dot(resid[p], inv[p], NT)
        return carry
    lax.fori_loop(0, panels, leaf_scale, 0)
    for e in range(sep_rows):
        c_hi[e], c_lo[e] = halved(coup[e])
        d_hi[e], d_lo[e] = halved(sinv[e])

    for e in range(sep_rows):
        for h in range(halves):
            m = e * halves + h
            lanes = slice(h * block, (h + 1) * block)
            drive[e, :, lanes] = sep[e, :, lanes] - (keep[0, m] + pair_recv[0, m].astype(F32))
    for d in order:
        if d > 0:
            chip_copy(d).wait_recv()
            for e in range(sep_rows):
                for h in range(halves):
                    lanes = slice(h * block, (h + 1) * block)
                    drive[e, :, lanes] = drive[e, :, lanes] - chip_recv[d, e * halves + h].astype(F32)

    rows_each = fields // SPLIT
    pieces = [(e, q) for e in range(sep_rows) for q in range(SPLIT)]

    def f_copy(i):
        return remote(f_send.at[i], f_recv.at[i], fs_sem.at[i], fr_sem.at[i], {"col": col + 1})

    def b_copy(i):
        return remote(b_send.at[i], b_recv.at[i], bs_sem.at[i], br_sem.at[i], {"col": col - 1})

    for i, (e, q) in enumerate(pieces):
        rows = slice(q * rows_each, (q + 1) * rows_each)

        @pl.when(has_below)
        def _(i=i, e=e, rows=rows):
            f_copy(i).wait_recv()
            drive[e, rows] = drive[e, rows] - (
                dot(f_recv[i], c_hi[e], NT) + dot(f_recv[i], c_lo[e], NT)
            )

        @pl.when(has_above)
        def _(i=i, e=e, rows=rows):
            f_send[i] = drive[e, rows].astype(BF16)
            f_copy(i).start()

        high, low = halved(drive[e, rows])
        scaled[e, rows] = dot(high, d_hi[e], NT) + dot(high, d_lo[e], NT) + dot(low, d_hi[e], NT)

    def spot(owner_leaf, e):
        return pl.ds((owner_leaf * sep_rows + e) * halves, halves)

    def gather_copy(d, e):
        here = gath.at[spot(leaf, e)]
        return remote(here, here, gs_sem.at[d, e], gr_sem.at[d, e], {"leaf": peer_chip[d] * 2 + core})

    def hand_copy(d, e):
        here = gath.at[spot(peer_chip[d] * 2 + core, e)]
        return remote(here, here, hs_sem.at[d, e], hr_sem.at[d, e], {"leaf": sibling})

    for i, (e, q) in enumerate(pieces):
        rows = slice(q * rows_each, (q + 1) * rows_each)

        @pl.when(has_above)
        def _(i=i, e=e, rows=rows):
            b_copy(i).wait_recv()
            scaled[e, rows] = scaled[e, rows] - b_recv[i].astype(F32)

        value = scaled[e, rows]
        low = value.astype(BF16)

        @pl.when(has_below)
        def _(i=i, e=e, value=value, low=low):
            rest = (value - low.astype(F32)).astype(BF16)
            up = dot(low, c_hi[e], NN) + dot(low, c_lo[e], NN) + dot(rest, c_hi[e], NN)
            b_send[i] = up.astype(b_send.dtype)
            b_copy(i).start()

        res[e, rows] = value
        for h in range(halves):
            gath[(leaf * sep_rows + e) * halves + h, rows] = low[:, h * block:(h + 1) * block]
        if q == SPLIT - 1:
            for d in order:
                if d > 0:
                    gather_copy(d, e).start()
            hand_copy(0, e).start()

    for e in range(sep_rows):
        for d in range(1, chips):
            gather_copy(d, e).wait_recv()
            hand_copy(d, e).start()
    for e in range(sep_rows):
        for d in range(chips):
            hand_copy(d, e).wait_recv()

    def correct(p, carry):
        one = gath[tab[2 * owners_cap + 2 * p]]
        two = gath[tab[2 * owners_cap + 2 * p + 1]]
        out[p] = out[p] - (dot(one, upd[p, :block], NN) + dot(two, upd[p, block:], NN))
        return carry
    lax.fori_loop(0, panels, correct, 0)

    for has, copy in ((has_below, z_down), (has_above, z_up), (leaf_below, x_down), (leaf_above, x_up)):
        @pl.when(has)
        def _(copy=copy):
            copy().wait_send()
    for i in range(len(pieces)):
        @pl.when(has_above)
        def _(i=i):
            f_copy(i).wait_send()

        @pl.when(has_below)
        def _(i=i):
            b_copy(i).wait_send()
    for d in range(chips):
        pair_copy(d).wait_send()
        if d > 0:
            chip_copy(d).wait_send()
        for e in range(sep_rows):
            hand_copy(d, e).wait_send()
            if d > 0:
                gather_copy(d, e).wait_send()


def body(
    voltage,
    source,
    conduct,
    leaf_inverse,
    update_rows,
    update_matrix,
    chain_slot,
    separator_source,
    separator_inverse,
    separator_coupling,
):
    fields, extent_x, extent_y, width = voltage.shape
    per_leaf = update_rows.shape[3]
    block = update_matrix.shape[2] // per_leaf
    halves = width // block
    panels = extent_x * extent_y
    chains = chain_slot.shape[0]
    sep_rows = separator_source.shape[1]
    n_leaf, n_col = lax.axis_size("leaf"), lax.axis_size("col")
    chips = n_leaf // 2
    entries = panels * per_leaf
    cap = max(2, (entries + n_leaf - 1) // n_leaf)
    local = sep_rows * halves

    targets = update_rows.reshape(entries)
    hit = (targets // halves)[:, None] == jnp.arange(chains, dtype=jnp.int32)
    slots = jnp.sum(jnp.where(hit, chain_slot, 0), axis=1)
    blocks = slots * halves + targets % halves
    owner = slots // sep_rows
    ids = jnp.arange(entries, dtype=jnp.int32)
    earlier = (owner[:, None] == owner[None, :]) & (ids[None, :] < ids[:, None])
    rank = jnp.sum(earlier.astype(jnp.int32), axis=1)
    place = owner * cap + rank
    at = jnp.arange(n_leaf * cap, dtype=jnp.int32)[:, None] == place[None, :]
    which = jnp.sum(jnp.where(at, ids, 0), axis=1)
    where = jnp.sum(jnp.where(at, blocks % local + 1, 0), axis=1) - 1
    table = jnp.concatenate([which, where, blocks]).astype(jnp.int32)

    v = jnp.transpose(voltage, (1, 2, 0, 3)).reshape(panels, fields, width)
    s = jnp.transpose(source, (1, 2, 0, 3)).reshape(panels, fields, width)
    sep = jnp.transpose(separator_source, (1, 0, 2))
    n_piece = sep_rows * SPLIT
    any_spec = pl.BlockSpec(memory_space=pl.ANY)
    vmem = pl.BlockSpec(memory_space=pltpu.VMEM)
    smem = pl.BlockSpec(memory_space=pltpu.SMEM)
    V, DMA = pltpu.VMEM, pltpu.SemaphoreType.DMA
    square = (sep_rows, width, width)
    leaf_out, sep_out = pl.pallas_call(
        functools.partial(kernel, n_leaf, n_col, cap, extent_x, extent_y, sep_rows, halves),
        out_shape=(
            jax.ShapeDtypeStruct((panels, fields, width), F32),
            jax.ShapeDtypeStruct((sep_rows, fields, width), F32),
        ),
        in_specs=[smem, vmem, vmem, vmem, vmem] + [any_spec] * 4,
        out_specs=(vmem, vmem),
        scratch_shapes=[
            V((panels, width, width), BF16), V((panels, width, width), BF16),
            V(square, F32), V(square, F32),
            V(square, BF16), V(square, BF16), V(square, BF16), V(square, BF16),
            V((panels, fields, width), BF16), V((entries, fields, block), F32),
            V((2, fields, 128), BF16), V((2, fields, 128), BF16),
            V((2, extent_y, fields, width), BF16),
            V((chips, local, fields, block), PAIR), V((chips, local, fields, block), PAIR),
            V((chips, local, fields, block), F32),
            V((chips, local, fields, block), BF16), V((chips, local, fields, block), BF16),
            V((sep_rows, fields, width), F32),
            V((n_piece, fields // SPLIT, width), BF16), V((n_piece, fields // SPLIT, width), BF16),
            V((sep_rows, fields, width), F32),
            V((n_piece, fields // SPLIT, width), HOP), V((n_piece, fields // SPLIT, width), HOP),
            V((n_leaf * local, fields, block), BF16),
            DMA((4,)), DMA((2,)), DMA((2,)), DMA((2,)), DMA((2,)),
            DMA((chips,)), DMA((chips,)), DMA((chips,)), DMA((chips,)),
            DMA((n_piece,)), DMA((n_piece,)), DMA((n_piece,)), DMA((n_piece,)),
            DMA((chips, sep_rows)), DMA((chips, sep_rows)),
            DMA((chips, sep_rows)), DMA((chips, sep_rows)),
        ],
        compiler_params=pltpu.CompilerParams(
            collective_id=0, has_side_effects=True, vmem_limit_bytes=56 * 2**20
        ),
    )(
        table, v, s, conduct.reshape(panels, width), sep,
        leaf_inverse.reshape(panels, width, width), update_matrix.reshape(panels, width, width),
        separator_inverse, separator_coupling,
    )
    leaf_result = jnp.transpose(
        leaf_out.reshape(extent_x, extent_y, fields, width), (2, 0, 1, 3)
    )
    return (leaf_result, jnp.transpose(sep_out, (1, 0, 2)))


def solution(mesh):
    placed = (
        P(None, "leaf", None, "col"),
        P(None, "leaf", None, "col"),
        P("leaf", None, "col"),
        P("leaf", None, "col", None),
        P("col", "leaf", None, None),
        P("leaf", None, None, "col"),
        P(),
        P(None, "leaf", "col"),
        P("leaf", "col", None),
        P("leaf", "col", None),
    )
    return jax.shard_map(
        body,
        mesh=mesh,
        in_specs=placed,
        out_specs=(P(None, "leaf", None, "col"), P(None, "leaf", "col")),
        check_vma=False,
    )
```

time: 201 us -> 70.3 us (0.35)
  waiting for transfers between devices: 98.7 us -> 0 us
  Pallas kernels: 0 us -> 54.5 us
  starting transfers between devices: 35.8 us -> 0 us
  matrix products: 19.6 us -> 0 us
  between operations: 14.3 us -> 0.68 us
  other arithmetic: 14 us -> 1.75 us
  local copies, waits for them, and re-layouts: 17 us -> 13 us
    pallas_call x0 -> x1, Pallas kernels: none -> 54.5 us  [body(): pl.pallas_call(functools.partial(kernel, n_leaf, n_col, cap, extent_x, ex...]
    ppermute x10 -> x0, waiting for transfers between devices: 45.7 us -> none  [the longest x6 32 us: shifted(): return lax.ppermute(block, axis, route)]
    all_gather x1 -> x0, waiting for transfers between devices: 32 us -> none  [body(): shard_piece = lax.all_gather(separator_low, 'leaf', axis=0, tiled=True)]
    ppermute x10 -> x0, starting transfers between devices: 26.8 us -> none  [the longest x6 13.9 us: shifted(): return lax.ppermute(block, axis, route)]
    all_to_all x2 -> x0, waiting for transfers between devices: 21 us -> none  [the longest x1 21 us: body(): lax.all_to_all(outgoing, 'leaf', split_axis=0, concat_axis=0, tiled=True)]
    dot_general x13 -> x0, matrix products: 19.6 us -> none  [the longest x1 5.1 us: body(): jnp.einsum('dce,enj->dcnj', selector, flat_contrib, precision=highest)]
    all_to_all x2 -> x0, starting transfers between devices: 8.78 us -> none  [the longest x1 4.43 us: body(): lax.all_to_all(outgoing, 'leaf', split_axis=0, concat_axis=0, tiled=True)]
    convert_element_type x7 -> x0, other arithmetic: 8.76 us -> none  [the longest x1 4.3 us: body(): residual.astype(jnp.bfloat16).reshape(fields, panels, panel_width)]
  transfers between devices with their start and end apart: 13 -> 0, of which waited for: 11 -> 0; matrix products, arithmetic and copies ran while one was open for 11% -> 0% of each run, Pallas kernels for 0% -> 0%
where the time goes in v1:
time: 70.3 us; the launch traced here: 70 us
  Pallas kernels  54.5 us (78%)
  local copies, waits for them, and re-layouts  13 us (18%)
  other arithmetic  1.75 us (2%)
    pallas_call x1, Pallas kernels, body(): pl.pallas_call(functools.partial(kernel, n_leaf, n_col, cap, extent_x, ex...  54.5 us
    reshape x1, local copies, waits for them, and re-layouts, body(): leaf_out.reshape(extent_x, extent_y, fields, width)  4.3 us
    unnamed x7, local copies, waits for them, and re-layouts  3.46 us
    transpose x1, local copies, waits for them, and re-layouts, body(): v = jnp.transpose(voltage, (1, 2, 0, 3)).reshape(panels, fields, width)  2.54 us

profile of v1, /device:TPU:1, one launch (start us, length us, event | category | flops | bytes accessed | tf_op | source)
XLA Modules:
  0.0 70.0 jit_solution(312268124717447269)
XLA Ops:
  0.6 0.0 copy-start
  0.6 0.9 %copy.24 = s32[1,4,4,2]{3,2,1,0:T(4,128)S(1)} copy(s32[1,4,4,2]{2,3,1,0:T(2,128)} %param.14) | data formatting | bytes 256 | tf_op args[4]
  1.5 0.1 reshape.93
  1.6 0.7 %select_reduce_fusion.2 = s32[32]{0:T(128)S(1)} fusion(s32[16]{0:T(128)} %param.16, s32[32]{0:T(128)S(1)} %and_select_fusion.3), kind=kLoop, calls=%fused_computation.8 | loop fusion | flops 1504 | bytes 320 | tf_op jit(solution)/shard_map/reduce_sum | solution.py:361
  2.4 0.2 convert_reduce_fusion
  2.6 0.1 select_reduce_fusion.1
  2.7 0.7 pad_add_fusion.tab
  3.4 1.3 %reshape.96.cond = f32[16,256]{1,0:T(8,128)} reshape(f32[4,4,256]{2,1,0:T(4,128)} %param.12) | data formatting | bytes 32768 | tf_op jit(solution)/shard_map/reshape | solution.py:415
  4.7 1.7 %copy.33 = f32[128,2,256]{2,0,1:T(8,128)} copy(f32[128,2,256]{2,1,0:T(2,128)} %param.17) | data formatting | bytes 524288 | tf_op args[7]
  6.4 2.5 %copy.25 = bf16[4,4,128,256]{3,2,1,0:T(8,128)(2,1)} copy(bf16[4,4,128,256]{3,1,0,2:T(4,128)(2,1)} %bitcast.21) | data formatting | bytes 2097152 | tf_op jit(solution)/shard_map/transpose | solution.py:373
  8.9 0.0 copy-done
  8.9 1.3 %copy.26 = bf16[4,4,128,256]{3,2,1,0:T(8,128)(2,1)} copy(bf16[4,4,128,256]{3,1,0,2:T(4,128)(2,1)S(1)} %bitcast.22) | data formatting | bytes 2097152 | tf_op jit(solution)/shard_map/transpose | solution.py:374
  10.2 54.5 %shard_map.113 = (f32[16,128,256]{2,1,0:T(8,128)}, f32[2,128,256]{2,1,0:T(8,128)}) custom-call(s32[96]{0:T(128)} %pad_add_fusion.tab, bf16[16,128,256]{2,1,0:T(8,128)(2,1)} %bitcast.14, bf16[16,128,256]{2,1,0:T(8,128)(2,1)} %bitcast.15, f32[16,256]{1,0:T(8,128)} %reshape.96.cond, f32[2,128,256]{2,1,0:T(8,128)} %bitcast.20, bf16[16,256,256]{2,1,0:T(8,128)(2,1)} %bitcast.18, ...), custom_call_target="tpu_custom_call" | custom-call | tf_op jit(solution)/shard_map/pallas_call | solution.py:382
  64.7 0.0 copy-start.1
  64.8 4.3 %copy.32 = f32[4,4,128,256]{3,1,0,2:T(4,128)} copy(f32[4,4,128,256]{3,2,1,0:T(8,128)} %bitcast.17) | data formatting | bytes 4194304 | tf_op jit(solution)/shard_map/reshape | solution.py:420
  69.1 0.0 copy-done.1
  69.1 0.9 %copy.29 = f32[128,2,256]{2,1,0:T(2,128)} copy(f32[128,2,256]{2,0,1:T(8,128)S(1)} %bitcast.23) | data formatting | bytes 524288
  (4 shorter events, 0.0 us)
Async XLA Ops:
  0.6 8.3 %copy-start = (bf16[128,4,4,256]{3,2,1,0:T(4,128)(2,1)S(1)}, bf16[128,4,4,256]{3,2,1,0:T(4,128)(2,1)}, u32[]{:S(2)}) copy-start(bf16[128,4,4,256]{3,2,1,0:T(4,128)(2,1)} %param.11) | copy-start | bytes 3145732
  64.7 4.3 %copy-start.1 = (f32[2,128,256]{2,1,0:T(8,128)S(1)}, f32[2,128,256]{2,1,0:T(8,128)}, u32[]{:S(2)}) copy-start(f32[2,128,256]{2,1,0:T(8,128)} %get-tuple-element.5) | copy-start | bytes 786436

commit v2 on v1

--- a/solution.py
+++ b/solution.py
@@ -37,8 +37,8 @@
 def kernel(
     n_leaf, n_col, cap, extent_x, extent_y, sep_rows, halves,
     tab, v, s, cond, sep, inv_hbm, upd_hbm, sinv_hbm, coup_hbm,
-    out, res,
-    inv, upd, sinv, coup, c_hi, c_lo, d_hi, d_lo,
+    ls_hbm, res, gath_hbm,
+    out, inv, upd, sinv, coup, c_hi, c_lo, d_hi, d_lo,
     resid, contrib, z_send, z_recv, x_recv,
     pair_send, pair_recv, keep, chip_send, chip_recv,
     drive, f_send, f_recv, scaled, b_send, b_recv, gath,
@@ -147,7 +147,7 @@
             beside = beside + v[p - 1].astype(F32)
         if y < extent_y - 1:
             beside = beside + v[p + 1].astype(F32)
-        low = (s[p].astype(F32) - ((6.0 + cond[p:p + 1, :]) * center - beside)).astype(BF16)
+        low = (s[p].astype(F32) - ((6.0 + cond[x, y:y + 1, :]) * center - beside)).astype(BF16)
         resid[p] = low
         product = dot(low, upd[p], NT)
         contrib[2 * p] = product[:, :block]
@@ -212,6 +212,8 @@
         out[p] = dot(resid[p], inv[p], NT)
         return carry
     lax.fori_loop(0, panels, leaf_scale, 0)
+    scaled_out = pltpu.make_async_copy(out, ls_hbm, load_sem.at[4])
+    scaled_out.start()
     for e in range(sep_rows):
         c_hi[e], c_lo[e] = halved(coup[e])
         d_hi[e], d_lo[e] = halved(sinv[e])
@@ -220,7 +222,7 @@
         for h in range(halves):
             m = e * halves + h
             lanes = slice(h * block, (h + 1) * block)
-            drive[e, :, lanes] = sep[e, :, lanes] - (keep[0, m] + pair_recv[0, m].astype(F32))
+            drive[e, :, lanes] = sep[:, e, lanes] - (keep[0, m] + pair_recv[0, m].astype(F32))
     for d in order:
         if d > 0:
             chip_copy(d).wait_recv()
@@ -238,24 +240,6 @@
     def b_copy(i):
         return remote(b_send.at[i], b_recv.at[i], bs_sem.at[i], br_sem.at[i], {"col": col - 1})
 
-    for i, (e, q) in enumerate(pieces):
-        rows = slice(q * rows_each, (q + 1) * rows_each)
-
-        @pl.when(has_below)
-        def _(i=i, e=e, rows=rows):
-            f_copy(i).wait_recv()
-            drive[e, rows] = drive[e, rows] - (
-                dot(f_recv[i], c_hi[e], NT) + dot(f_recv[i], c_lo[e], NT)
-            )
-
-        @pl.when(has_above)
-        def _(i=i, e=e, rows=rows):
-            f_send[i] = drive[e, rows].astype(BF16)
-            f_copy(i).start()
-
-        high, low = halved(drive[e, rows])
-        scaled[e, rows] = dot(high, d_hi[e], NT) + dot(high, d_lo[e], NT) + dot(low, d_hi[e], NT)
-
     def spot(owner_leaf, e):
         return pl.ds((owner_leaf * sep_rows + e) * halves, halves)
 
@@ -267,19 +251,15 @@
         here = gath.at[spot(peer_chip[d] * 2 + core, e)]
         return remote(here, here, hs_sem.at[d, e], hr_sem.at[d, e], {"leaf": sibling})
 
-    for i, (e, q) in enumerate(pieces):
-        rows = slice(q * rows_each, (q + 1) * rows_each)
-
-        @pl.when(has_above)
-        def _(i=i, e=e, rows=rows):
-            b_copy(i).wait_recv()
-            scaled[e, rows] = scaled[e, rows] - b_recv[i].astype(F32)
-
-        value = scaled[e, rows]
+    def scale(e, rows):
+        high, low = halved(drive[e, rows])
+        return dot(high, d_hi[e], NT) + dot(high, d_lo[e], NT) + dot(low, d_hi[e], NT)
+
+    def settle(i, e, q, rows, value):
         low = value.astype(BF16)
 
         @pl.when(has_below)
-        def _(i=i, e=e, value=value, low=low):
+        def _():
             rest = (value - low.astype(F32)).astype(BF16)
             up = dot(low, c_hi[e], NN) + dot(low, c_lo[e], NN) + dot(rest, c_hi[e], NN)
             b_send[i] = up.astype(b_send.dtype)
@@ -294,6 +274,34 @@
                     gather_copy(d, e).start()
             hand_copy(0, e).start()
 
+    for i, (e, q) in enumerate(pieces):
+        rows = slice(q * rows_each, (q + 1) * rows_each)
+
+        @pl.when(has_below)
+        def _(i=i, e=e, rows=rows):
+            f_copy(i).wait_recv()
+            drive[e, rows] = drive[e, rows] - (
+                dot(f_recv[i], c_hi[e], NT) + dot(f_recv[i], c_lo[e], NT)
+            )
+
+        @pl.when(has_above)
+        def _(i=i, e=e, rows=rows):
+            f_send[i] = drive[e, rows].astype(BF16)
+            f_copy(i).start()
+
+        @pl.when(jnp.logical_not(has_above))
+        def _(i=i, e=e, q=q, rows=rows):
+            settle(i, e, q, rows, scale(e, rows))
+
+    @pl.when(has_above)
+    def _():
+        for e in range(sep_rows):
+            scaled[e] = scale(e, slice(None))
+        for i, (e, q) in enumerate(pieces):
+            rows = slice(q * rows_each, (q + 1) * rows_each)
+            b_copy(i).wait_recv()
+            settle(i, e, q, rows, scaled[e, rows] - b_recv[i].astype(F32))
+
     for e in range(sep_rows):
         for d in range(1, chips):
             gather_copy(d, e).wait_recv()
@@ -302,13 +310,8 @@
         for d in range(chips):
             hand_copy(d, e).wait_recv()
 
-    def correct(p, carry):
-        one = gath[tab[2 * owners_cap + 2 * p]]
-        two = gath[tab[2 * owners_cap + 2 * p + 1]]
-        out[p] = out[p] - (dot(one, upd[p, :block], NN) + dot(two, upd[p, block:], NN))
-        return carry
-    lax.fori_loop(0, panels, correct, 0)
-
+    gath_out = pltpu.make_async_copy(gath, gath_hbm, load_sem.at[5])
+    gath_out.start()
     for has, copy in ((has_below, z_down), (has_above, z_up), (leaf_below, x_down), (leaf_above, x_up)):
         @pl.when(has)
         def _(copy=copy):
@@ -329,6 +332,18 @@
             hand_copy(d, e).wait_send()
             if d > 0:
                 gather_copy(d, e).wait_send()
+    scaled_out.wait()
+    gath_out.wait()
+
+
+def finish(start, tab, upd, gath, ls, out):
+    extent_y, fields, width = ls.shape
+    block = gath.shape[2]
+    x = pl.program_id(0)
+    for y in range(extent_y):
+        at = start + 2 * (x * extent_y + y)
+        total = dot(gath[tab[at]], upd[y, :block], NN) + dot(gath[tab[at + 1]], upd[y, block:], NN)
+        out[:, 0, y, :] = ls[y] - total
 
 
 def body(
@@ -372,22 +387,23 @@
 
     v = jnp.transpose(voltage, (1, 2, 0, 3)).reshape(panels, fields, width)
     s = jnp.transpose(source, (1, 2, 0, 3)).reshape(panels, fields, width)
-    sep = jnp.transpose(separator_source, (1, 0, 2))
     n_piece = sep_rows * SPLIT
     any_spec = pl.BlockSpec(memory_space=pl.ANY)
     vmem = pl.BlockSpec(memory_space=pltpu.VMEM)
     smem = pl.BlockSpec(memory_space=pltpu.SMEM)
     V, DMA = pltpu.VMEM, pltpu.SemaphoreType.DMA
     square = (sep_rows, width, width)
-    leaf_out, sep_out = pl.pallas_call(
+    ls, sep_out, gathered = pl.pallas_call(
         functools.partial(kernel, n_leaf, n_col, cap, extent_x, extent_y, sep_rows, halves),
         out_shape=(
             jax.ShapeDtypeStruct((panels, fields, width), F32),
             jax.ShapeDtypeStruct((sep_rows, fields, width), F32),
+            jax.ShapeDtypeStruct((n_leaf * local, fields, block), BF16),
         ),
         in_specs=[smem, vmem, vmem, vmem, vmem] + [any_spec] * 4,
-        out_specs=(vmem, vmem),
+        out_specs=(any_spec, vmem, any_spec),
         scratch_shapes=[
+            V((panels, fields, width), F32),
             V((panels, width, width), BF16), V((panels, width, width), BF16),
             V(square, F32), V(square, F32),
             V(square, BF16), V(square, BF16), V(square, BF16), V(square, BF16),
@@ -402,7 +418,7 @@
             V((sep_rows, fields, width), F32),
             V((n_piece, fields // SPLIT, width), HOP), V((n_piece, fields // SPLIT, width), HOP),
             V((n_leaf * local, fields, block), BF16),
-            DMA((4,)), DMA((2,)), DMA((2,)), DMA((2,)), DMA((2,)),
+            DMA((6,)), DMA((2,)), DMA((2,)), DMA((2,)), DMA((2,)),
             DMA((chips,)), DMA((chips,)), DMA((chips,)), DMA((chips,)),
             DMA((n_piece,)), DMA((n_piece,)), DMA((n_piece,)), DMA((n_piece,)),
             DMA((chips, sep_rows)), DMA((chips, sep_rows)),
@@ -412,13 +428,23 @@
             collective_id=0, has_side_effects=True, vmem_limit_bytes=56 * 2**20
         ),
     )(
-        table, v, s, conduct.reshape(panels, width), sep,
+        table, v, s, conduct, separator_source,
         leaf_inverse.reshape(panels, width, width), update_matrix.reshape(panels, width, width),
         separator_inverse, separator_coupling,
     )
-    leaf_result = jnp.transpose(
-        leaf_out.reshape(extent_x, extent_y, fields, width), (2, 0, 1, 3)
-    )
+    leaf_result = pl.pallas_call(
+        functools.partial(finish, 2 * n_leaf * cap),
+        out_shape=jax.ShapeDtypeStruct((fields, extent_x, extent_y, width), F32),
+        grid=(extent_x,),
+        in_specs=[
+            smem,
+            pl.BlockSpec((extent_y, width, width), lambda x: (x, 0, 0)),
+            vmem,
+            pl.BlockSpec((extent_y, fields, width), lambda x: (x, 0, 0)),
+        ],
+        out_specs=pl.BlockSpec((fields, 1, extent_y, width), lambda x: (0, x, 0, 0)),
+        compiler_params=pltpu.CompilerParams(vmem_limit_bytes=56 * 2**20),
+    )(table, update_matrix.reshape(panels, width, width), gathered, ls)
     return (leaf_result, jnp.transpose(sep_out, (1, 0, 2)))
 
 

time: 70.3 us -> 64.3 us (0.915)
  local copies, waits for them, and re-layouts: 13 us -> 5.74 us
  Pallas kernels: 54.5 us -> 56 us
    reshape x2 -> x0, local copies, waits for them, and re-layouts: 5.62 us -> none  [the longest x1 4.3 us: body(): leaf_out.reshape(extent_x, extent_y, fields, width)]
    pallas_call x0 -> x1, Pallas kernels: none -> 5.19 us  [body(): pl.pallas_call(functools.partial(finish, 2 * n_leaf * cap), out_shape=jax...]
    pallas_call x1, Pallas kernels: 54.5 us -> 50.8 us  [body(): pl.pallas_call(functools.partial(kernel, n_leaf, n_col, cap, extent_x, ex...]
    unnamed x7 -> x6, local copies, waits for them, and re-layouts: 3.46 us -> 1.79 us
where the time goes in v2:
time: 64.3 us; the launch traced here: 64.1 us
  Pallas kernels  56 us (87%)
  local copies, waits for them, and re-layouts  5.74 us (9%)
  other arithmetic  1.67 us (3%)
  between operations  0.68 us (1%)
    pallas_call x1, Pallas kernels, body(): pl.pallas_call(functools.partial(kernel, n_leaf, n_col, cap, extent_x, ex...  50.8 us
    pallas_call x1, Pallas kernels, body(): pl.pallas_call(functools.partial(finish, 2 * n_leaf * cap), out_shape=jax...  5.19 us
    transpose x1, local copies, waits for them, and re-layouts, body(): v = jnp.transpose(voltage, (1, 2, 0, 3)).reshape(panels, fields, width)  2.54 us
    unnamed x6, local copies, waits for them, and re-layouts  1.79 us
    transpose x1, local copies, waits for them, and re-layouts, body(): s = jnp.transpose(source, (1, 2, 0, 3)).reshape(panels, fields, width)  1.32 us

profile of v2, /device:TPU:1, one launch (start us, length us, event | category | flops | bytes accessed | tf_op | source)
XLA Modules:
  0.0 64.1 jit_solution(13787526413331828703)
XLA Ops:
  0.6 0.0 copy-start
  0.6 0.9 %copy.20 = s32[1,4,4,2]{3,2,1,0:T(4,128)S(1)} copy(s32[1,4,4,2]{2,3,1,0:T(2,128)} %param.14) | data formatting | bytes 256 | tf_op args[4]
  1.5 0.1 reshape.88
  1.6 0.7 %select_reduce_fusion.2 = s32[32]{0:T(128)S(1)} fusion(s32[16]{0:T(128)} %param.16, s32[32]{0:T(128)S(1)} %and_select_fusion.3), kind=kLoop, calls=%fused_computation.6 | loop fusion | flops 1504 | bytes 320 | tf_op jit(solution)/shard_map/reduce_sum | solution.py:376
  2.4 0.2 convert_reduce_fusion
  2.6 0.1 select_reduce_fusion.1
  2.7 0.6 pad_add_fusion.tab
  3.3 2.5 %copy.21 = bf16[4,4,128,256]{3,2,1,0:T(8,128)(2,1)} copy(bf16[4,4,128,256]{3,1,0,2:T(4,128)(2,1)} %bitcast.12) | data formatting | bytes 2097152 | tf_op jit(solution)/shard_map/transpose | solution.py:388
  5.8 0.0 copy-done
  5.8 1.3 %copy.22 = bf16[4,4,128,256]{3,2,1,0:T(8,128)(2,1)} copy(bf16[4,4,128,256]{3,1,0,2:T(4,128)(2,1)S(1)} %bitcast.13) | data formatting | bytes 2097152 | tf_op jit(solution)/shard_map/transpose | solution.py:389
  7.2 50.8 %shard_map.113 = (f32[16,128,256]{2,1,0:T(8,128)}, f32[2,128,256]{2,1,0:T(8,128)}, bf16[32,128,128]{2,1,0:T(8,128)(2,1)}) custom-call(s32[96]{0:T(128)} %pad_add_fusion.tab, bf16[16,128,256]{2,1,0:T(8,128)(2,1)} %bitcast.9, bf16[16,128,256]{2,1,0:T(8,128)(2,1)} %bitcast.10, f32[4,4,256]{2,1,0:T(4,128)} %cond.1, f32[128,2,256]{2,1,0:T(2,128)} %sep.1, ...), custom_call_target="tpu_custom_call" | custom-call | tf_op jit(solution)/shard_map/pallas_call | solution.py:396
  58.0 0.0 copy-start.1
  58.0 5.2 %shard_map.114 = f32[128,4,4,256]{3,2,1,0:T(4,128)} custom-call(s32[96]{0:T(128)} %pad_add_fusion.tab, bf16[16,256,256]{2,1,0:T(8,128)(2,1)} %bitcast.8, bf16[32,128,128]{2,1,0:T(8,128)(2,1)} %get-tuple-element.5.gath, f32[16,128,256]{2,1,0:T(8,128)} %get-tuple-element.6.ls), custom_call_target="tpu_custom_call" | custom-call | tf_op jit(solution)/shard_map/pallas_call | solution.py:435
  63.2 0.0 copy-done.1
  63.2 0.9 %copy.23 = f32[128,2,256]{2,1,0:T(2,128)} copy(f32[128,2,256]{2,0,1:T(8,128)S(1)} %bitcast.14) | data formatting | bytes 524288
  (4 shorter events, 0.0 us)
Async XLA Ops:
  0.6 5.2 %copy-start = (bf16[128,4,4,256]{3,2,1,0:T(4,128)(2,1)S(1)}, bf16[128,4,4,256]{3,2,1,0:T(4,128)(2,1)}, u32[]{:S(2)}) copy-start(bf16[128,4,4,256]{3,2,1,0:T(4,128)(2,1)} %param.11) | copy-start | bytes 3145732
  58.0 5.2 %copy-start.1 = (f32[2,128,256]{2,1,0:T(8,128)S(1)}, f32[2,128,256]{2,1,0:T(8,128)}, u32[]{:S(2)}) copy-start(f32[2,128,256]{2,1,0:T(8,128)} %get-tuple-element.7) | copy-start | bytes 786436
